TPU v7x, 32 devices: a whole 2x2x4 slice. The times are simulated.
32 devices in a mesh: sy: 4 (over z), sx: 4 (over y, core), tp: 2 (over x).
Axes of the slice: x: 2, y: 2, z: 4, core: 2. Of those that a mesh axis runs over, the one named last changes fastest.
Arguments:
- features: bfloat16 [96, 64, 1408], P('sy', 'sx', 'tp'), may hold values from -6 to 6
- depth_kernel: float32 [7, 7, 1408], P(None, None, 'tp'), may hold values from -0.875 to 0.875
- depth_bias: float32 [1408], P('tp'), may hold values from -1 to 1
- norm_gain: float32 [1408], replicated, may hold values from 0.1 to 1.9
- norm_bias: float32 [1408], replicated, may hold values from -3 to 3
- up_weight: bfloat16 [1408, 5632], P(None, 'tp'), may hold values from -0.15625 to 0.15625
- up_bias: float32 [5632], P('tp'), may hold values from -3 to 3
- response_gain: float32 [5632], P('tp'), may hold values from -4 to 4
- response_shift: float32 [5632], P('tp'), may hold values from -3 to 3
- down_weight: bfloat16 [5632, 1408], P('tp', ('sy', 'sx')), may hold values from -0.078125 to 0.078125
- down_bias: float32 [1408], P('tp'), may hold values from -3 to 3
- tissue: int32 [12, 8], P('sy', 'sx'), may hold values from 0 to 1, as said below
- cotangent: bfloat16 [96, 64, 1408], P('sy', 'sx', 'tp'), may hold values from -6 to 6
Outputs:
- block_out: bfloat16 [96, 64, 1408], P('sy', 'sx', 'tp')
- feature_grad: bfloat16 [96, 64, 1408], P('sy', 'sx', 'tp')
Inputs may be any that keep to these rules, and one draw needn't show every extreme that they name: Each device's block of 3 x 2 tiles holds 1 to 4 tissue tiles; some device's block holds exactly 4.
All inputs are finite; a program needn't handle non-finite values.
Results may differ from a plain program's by a relative error of at most 0.0049.
The roundings to bfloat16 on the way count: a program that leaves them out, or rounds other values in their place, can miss the bound.
Values may be sent and summed in bfloat16 or wider, within the bound.
A program may use at most 128 MiB of HBM per device.

v0:
```python
import jax
import jax.numpy as jnp
from jax import lax
from jax.sharding import PartitionSpec as P

KERNEL = 7
TILE = 8
root_half = 0.7071067811865476
root_two_pi_inv = 0.3989422804014327


def extended(block, sides, width):
    for axis, dim in sides:
        count = lax.axis_size(axis)
        forward = [(i, i + 1) for i in range(count - 1)]
        backward = [(target, source) for source, target in forward]
        low = lax.ppermute(
            lax.slice_in_dim(block, block.shape[dim] - width, None, axis=dim), axis, forward
        )
        high = lax.ppermute(lax.slice_in_dim(block, 0, width, axis=dim), axis, backward)
        block = jnp.concatenate([low, block, high], axis=dim)
    return block


def gelu_value(values):
    return 0.5 * values * (1.0 + jax.scipy.special.erf(values * root_half))


def gelu_slope(values):
    return (
        0.5 * (1.0 + jax.scipy.special.erf(values * root_half))
        + values * jnp.exp(-0.5 * values * values) * root_two_pi_inv
    )


def depthwise(padded, kernel, rows_out, cols_out, flipped):
    summed = jnp.zeros((rows_out, cols_out, kernel.shape[2]), jnp.float32)
    last_tap = KERNEL - 1
    for row_tap in range(KERNEL):
        for col_tap in range(KERNEL):
            row_start = last_tap - row_tap if flipped else row_tap
            col_start = last_tap - col_tap if flipped else col_tap
            window = padded[row_start : row_start + rows_out, col_start : col_start + cols_out]
            summed = summed + window.astype(jnp.float32) * kernel[row_tap, col_tap]
    return summed


MOST = 4


def extend(image):
    return extended(image, (("sy", 0), ("sx", 1)), KERNEL // 2)


def swapped(array):
    count = lax.axis_size("tp")
    return lax.ppermute(array, "tp", [(i, count - 1 - i) for i in range(count)])


def over_pixels(vector):
    return lax.psum(vector, ("sy", "sx"))


def conv_tiles(windows, kernel):
    summed = jnp.zeros((windows.shape[0], TILE, TILE, windows.shape[3]), jnp.float32)
    for row_tap in range(KERNEL):
        for col_tap in range(KERNEL):
            window = windows[:, row_tap : row_tap + TILE, col_tap : col_tap + TILE]
            summed = summed + window.astype(jnp.float32) * kernel[row_tap, col_tap]
    return summed


def shards(
    features,
    depth_kernel,
    depth_bias,
    norm_gain,
    norm_bias,
    up_weight,
    up_bias,
    response_gain,
    response_shift,
    down_weight,
    down_bias,
    tissue,
    cotangent,
):
    image_rows, image_cols, local_channels = features.shape
    tiles_y, tiles_x = tissue.shape
    tiles = tiles_y * tiles_x
    channels = up_weight.shape[0]
    hidden_total = up_weight.shape[1] * lax.axis_size("tp")
    tp_index = lax.axis_index("tp")
    first = tp_index == 0
    channel_start = tp_index * local_channels
    other_start = (1 - tp_index) * local_channels
    contract_last = (((1,), (1,)), ((), ()))
    pixels = MOST * TILE * TILE
    down_t = lax.all_gather(down_weight.T, ("sy", "sx"), axis=0, tiled=True)
    flags = tissue.reshape(-1)
    tile_ids = jnp.arange(tiles, dtype=jnp.int32)
    earlier = (tile_ids[None, :] < tile_ids[:, None]).astype(jnp.int32)
    ahead = jnp.sum(earlier * flags[None, :], axis=1)
    slot_of = jnp.where(flags > 0, ahead, jnp.sum(flags) + tile_ids - ahead)
    chosen = [jnp.sum(jnp.where(slot_of == s, tile_ids, 0)) for s in range(MOST)]
    slot_mask = jnp.stack([jnp.sum(jnp.where(slot_of == s, flags, 0)) for s in range(MOST)])
    mask_rows = jnp.repeat(slot_mask, TILE * TILE).astype(jnp.float32)

    def windows_of(image, side):
        return jnp.stack(
            [
                lax.dynamic_slice(
                    image,
                    (t // tiles_x * TILE, t % tiles_x * TILE, 0),
                    (side, side, image.shape[2]),
                )
                for t in chosen
            ]
        )

    def spread_out(rows_array):
        held = rows_array.reshape(MOST, TILE, TILE, rows_array.shape[1])
        held = jnp.concatenate([held, jnp.zeros_like(held[:1])], axis=0)
        slots = jnp.minimum(slot_of, MOST)
        rows = []
        for ty in range(tiles_y):
            row = [
                lax.dynamic_index_in_dim(held, slots[ty * tiles_x + tx], 0, keepdims=False)
                for tx in range(tiles_x)
            ]
            rows.append(jnp.concatenate(row, axis=1))
        return jnp.concatenate(rows, axis=0)

    def both_halves(own):
        other = swapped(own)
        return jnp.where(
            first, jnp.concatenate([own, other], axis=1), jnp.concatenate([other, own], axis=1)
        )

    cot_tiles = windows_of(cotangent, TILE).reshape(pixels, local_channels)
    masked_cot = (cot_tiles.astype(jnp.float32) * mask_rows[:, None]).astype(jnp.bfloat16)
    cot_wide = both_halves(masked_cot)
    convolved = conv_tiles(windows_of(extend(features), TILE + KERNEL - 1), depth_kernel)
    convolved = (convolved + depth_bias).astype(jnp.bfloat16).reshape(pixels, local_channels)
    gathered = both_halves(convolved).astype(jnp.float32)
    centre = jnp.mean(gathered, axis=1, keepdims=True)
    spread = jnp.mean(jnp.square(gathered - centre), axis=1, keepdims=True)
    inv_scale = lax.rsqrt(spread + 1e-06)
    standard = (gathered - centre) * inv_scale
    normed = (standard * norm_gain + norm_bias).astype(jnp.bfloat16)
    preact = jnp.dot(normed, up_weight, preferred_element_type=jnp.float32) + up_bias
    hidden = gelu_value(preact).astype(jnp.bfloat16)
    hidden_wide = hidden.astype(jnp.float32)
    squares = over_pixels(jnp.sum(mask_rows[:, None] * hidden_wide * hidden_wide, axis=0))
    column_norms = jnp.sqrt(squares)
    norms_here = jnp.full((8, 128), jnp.sum(column_norms))
    norm_level = (norms_here + swapped(norms_here))[0, 0] / hidden_total + 1e-06
    norm_ratio = column_norms / norm_level
    back_hidden = jnp.dot(cot_wide, down_t, preferred_element_type=jnp.float32)
    products = over_pixels(jnp.sum(back_hidden * hidden_wide, axis=0))
    response = (response_gain * hidden_wide * norm_ratio + response_shift + hidden_wide).astype(
        jnp.bfloat16
    )
    partial_out = lax.dot_general(
        response, down_t, contract_last, preferred_element_type=jnp.float32
    )
    sent_out = lax.dynamic_slice_in_dim(partial_out, other_start, local_channels, 1)
    kept_out = lax.dynamic_slice_in_dim(partial_out, channel_start, local_channels, 1)
    branch = kept_out + swapped(sent_out.astype(jnp.bfloat16)).astype(jnp.float32)
    ratio_grad = response_gain * products
    dots_here = jnp.full((8, 128), jnp.sum(ratio_grad * column_norms))
    dots = (dots_here + swapped(dots_here))[0, 0]
    norms_grad = ratio_grad / norm_level - dots / (hidden_total * norm_level * norm_level)
    hidden_grad = (
        back_hidden * (response_gain * norm_ratio + 1.0)
        + norms_grad * mask_rows[:, None] * hidden_wide / column_norms
    )
    preact_grad = (hidden_grad * gelu_slope(preact)).astype(jnp.bfloat16)
    grad_terms = lax.dot_general(
        preact_grad, up_weight, contract_last, preferred_element_type=jnp.float32
    )
    scaled_terms = grad_terms * norm_gain
    sums_here = jnp.stack([jnp.sum(scaled_terms, axis=1), jnp.sum(scaled_terms * standard, axis=1)])
    sums = sums_here + swapped(sums_here)
    sent_grad = lax.dynamic_slice_in_dim(scaled_terms, other_start, local_channels, 1)
    kept_grad = lax.dynamic_slice_in_dim(scaled_terms, channel_start, local_channels, 1)
    own_standard = lax.dynamic_slice_in_dim(standard, channel_start, local_channels, 1)
    scaled = kept_grad + swapped(sent_grad.astype(jnp.bfloat16)).astype(jnp.float32)
    convolved_grad = inv_scale * (
        scaled - (sums[0] / channels)[:, None] - own_standard * (sums[1] / channels)[:, None]
    )
    grad_image = spread_out(convolved_grad.astype(jnp.bfloat16))
    feature_grad = (
        cotangent.astype(jnp.float32)
        + depthwise(extend(grad_image), depth_kernel, image_rows, image_cols, True)
    ).astype(jnp.bfloat16)
    addend = spread_out(mask_rows[:, None] * (branch + down_bias))
    block_out = (features.astype(jnp.float32) + addend).astype(jnp.bfloat16)
    return (block_out, feature_grad)


def solution(mesh):
    placed = (
        P("sy", "sx", "tp"),
        P(None, None, "tp"),
        P("tp"),
        P(),
        P(),
        P(None, "tp"),
        P("tp"),
        P("tp"),
        P("tp"),
        P("tp", ("sy", "sx")),
        P("tp"),
        P("sy", "sx"),
        P("sy", "sx", "tp"),
    )
    return jax.shard_map(
        shards,
        mesh=mesh,
        in_specs=placed,
        out_specs=(P("sy", "sx", "tp"), P("sy", "sx", "tp")),
        check_vma=False,
    )
```

profile of v0, /device:TPU:12, one launch (start us, length us, event | category | flops | bytes accessed | tf_op | source)
XLA Modules:
  0.0 235.3 jit_solution(2763965542860036640)
XLA Ops:
  8.9 3.6 %collective-permute-start = (bf16[3,16,704]{2,1,0:T(8,128)(2,1)S(1)}, bf16[3,16,704]{2,1,0:T(8,128)(2,1)S(1)}, u32[]{:S(2)}, u32[]{:S(2)}) collective-permute-start(bf16[3,16,704]{2,1,0:T(8,128)(2,1)S(1)} %get-tuple-element.90), channel_id=1, source_target_pairs={{0,8},{8,16},{16,24},{1,9},{9,17},{17,25},{2,10},{10,18},{18,26},{... | collective-permute-start | bytes 202760 | tf_op jit(solution)/shard_map/ppermute | solution.py:17
  12.5 2.4 %collective-permute-start.1 = (bf16[3,16,704]{2,1,0:T(8,128)(2,1)S(1)}, bf16[3,16,704]{2,1,0:T(8,128)(2,1)S(1)}, u32[]{:S(2)}, u32[]{:S(2)}) collective-permute-start(bf16[3,16,704]{2,1,0:T(8,128)(2,1)S(1)} %get-tuple-element.89), channel_id=1, source_target_pairs={{8,0},{16,8},{24,16},{9,1},{17,9},{25,17},{10,2},{18,10},{26,18},{... | collective-permute-start | bytes 202760 | tf_op jit(solution)/shard_map/ppermute | solution.py:20
  28.8 2.7 %add_convert_fusion.4 = f32[4]{0:T(128)S(1)} fusion(s32[1]{0:T(128)} %bitcast.3, s32[1]{0:T(128)} %bitcast.2, s32[1]{0:T(128)} %bitcast.1, s32[1]{0:T(128)} %bitcast), kind=kLoop, calls=%fused_computation.313 | loop fusion | flops 16 | bytes 32 | tf_op jit(solution)/shard_map/convert_element_type | solution.py:107
  32.4 1.9 collective-permute-start.2
  34.3 3.6 %collective-permute-start.3 = (bf16[30,3,704]{2,1,0:T(4,128)(2,1)S(1)}, bf16[30,3,704]{2,1,0:T(4,128)(2,1)S(1)}, u32[]{:S(2)}, u32[]{:S(2)}) collective-permute-start(bf16[30,3,704]{2,1,0:T(4,128)(2,1)S(1)} %get-tuple-element.86), channel_id=1, source_target_pairs={{2,0},{4,2},{6,4},{3,1},{5,3},{7,5},{10,8},{12,10},{14,12},{11,9},... | collective-permute-start | bytes 380168 | tf_op jit(solution)/shard_map/ppermute | solution.py:20
  39.2 1.8 collective-permute-done.3
  43.0 5.8 %add_convert_fusion.2 = bf16[4,8,8,704]{3,2,1,0:T(8,128)(2,1)S(1)} fusion(bf16[4,14,14,704]{3,2,1,0:T(8,128)(2,1)S(1)} %pad_maximum_fusion, f32[704]{0:T(1024)S(1)} %copy-done.4, f32[704]{0:T(1024)S(1)} %get-tuple-element.53, f32[704]{0:T(1024)S(1)} %get-tuple-element.54, f32[704]{0:T(1024)S(1)} %get-tuple-element.7, f32[704]{0:T(1024)S(1)} %get-tuple-element.8, ...), kind=kLoop, calls=%fused_computation.138 | loop fusion | flops 26673152 | bytes 18163200 | tf_op jit(solution)/shard_map/convert_element_type | solution.py:144
  48.8 1.6 collective-permute-start.4
  51.8 9.1 %collective-permute-done.4 = bf16[256,704]{1,0:T(8,128)(2,1)S(1)} collective-permute-done((bf16[256,704]{1,0:T(8,128)(2,1)S(1)}, bf16[256,704]{1,0:T(8,128)(2,1)S(1)}, u32[]{:S(2)}, u32[]{:S(2)}) %collective-permute-start.4) | collective-permute-done | bytes 360480 | tf_op jit(solution)/shard_map/ppermute | solution.py:57
  62.2 7.7 %convolution_add_fusion = f32[256,2816]{1,0:T(8,128)} fusion(bf16[1408,2816]{1,0:T(8,128)(2,1)} %param.18, f32[2816]{0:T(1024)S(1)} %copy-done.6, f32[1408]{0:T(1024)S(1)} %copy-done.8, f32[1408]{0:T(1024)S(1)} %copy-done.9, f32[256]{0:T(256)S(1)} %add_rsqrt_fusion, f32[256]{0:T(256)S(1)} %broadcast_multiply_fusion, bf16[256,704]{1,0:T(8,128)(2,1)S(1)} %bitcast.70, ...), kind=kOutput, calls=%fused_computation.47 | convolution fusion | flops 2036170752 | bytes 11558913 | tf_op jit(solution)/shard_map/dot_general | solution.py:151
  69.9 12.2 %all-gather.2.cloned.1.call-done = bf16[1408,2816]{1,0:T(8,128)(2,1)} async-done(((bf16[88,2816]{1,0:T(8,128)(2,1)}), bf16[1408,2816]{1,0:T(8,128)(2,1)}) %all-gather.2.cloned.1.call-update) | async-done | bytes 7929872 | tf_op jit(solution)/shard_map/all_gather | solution.py:99
  82.0 8.3 %fusion.10 = (f32[2816]{0:T(1024)S(1)}, f32[2816]{0:T(1024)S(1)}, bf16[256,2816]{1,0:T(8,128)(2,1)}, f32[256,2816]{1,0:T(8,128)}) fusion(f32[256]{0:T(256)S(1)} %convert_element_type.365, f32[256,2816]{1,0:T(8,128)} %convolution_add_fusion, bf16[1408,2816]{1,0:T(8,128)(2,1)} %all-gather.2.cloned.1.call-done, ...), kind=kOutput, calls=%fused_computation.58 | convolution fusion | flops 2041211392 | bytes 15883265 | tf_op jit(solution)/shard_map/dot_general | solution.py:159
  90.3 48.0 %all-reduce.2 = (f32[2816]{0:T(1024)S(1)}, f32[2816]{0:T(1024)S(1)}) all-reduce(f32[2816]{0:T(1024)S(1)} %get-tuple-element.4, f32[2816]{0:T(1024)S(1)} %get-tuple-element.5), channel_id=1, replica_groups=mesh['sy'=4,'sx'=4,'tp'=2] {'sy','sx'}, use_global_device_ids=true, to_apply=%region_16.17 | all-reduce | flops 5632 | bytes 45056 | tf_op jit(solution)/shard_map/psum | solution.py:61
  139.7 1.4 collective-permute-start.5
  159.8 6.3 %fusion.16 = f32[256,1408]{1,0:T(8,128)S(1)} fusion(bf16[1408,2816]{1,0:T(8,128)(2,1)} %all-gather.2.cloned.1.call-done, bf16[256,2816]{1,0:T(8,128)(2,1)} %get-tuple-element.69, f32[2816]{0:T(1024)S(1)} %copy-done.7, f32[2816]{0:T(1024)S(1)} %get-tuple-element.68, f32[2816]{0:T(1024)S(1)} %copy-done.3), kind=kOutput, calls=%fused_computation.109 | convolution fusion | flops 2034368512 | bytes 10847232 | tf_op jit(solution)/shard_map/dot_general | solution.py:164
  167.0 6.9 %fusion.102 = (f32[256]{0:T(256)S(1)}, f32[256]{0:T(256)S(1)}, f32[256,1408]{1,0:T(8,128)S(1)}, f32[256,1408]{1,0:T(8,128)S(1)}) fusion(f32[256]{0:T(256)S(1)} %add_rsqrt_fusion, f32[256]{0:T(256)S(1)} %broadcast_multiply_fusion, bf16[256,704]{1,0:T(8,128)(2,1)S(1)} %bitcast.71, bf16[256,704]{1,0:T(8,128)(2,1)S(1)} %collective-permute-done.4, ...), kind=kOutput, calls=%fused_computation.322 | convolution fusion | flops 2047344128 | bytes 18787840 | tf_op jit(solution)/shard_map/dot_general | solution.py:179
  177.7 5.7 %collective-permute-done.9 = bf16[256,704]{1,0:T(8,128)(2,1)S(1)} collective-permute-done((bf16[256,704]{1,0:T(8,128)(2,1)S(1)}, bf16[256,704]{1,0:T(8,128)(2,1)S(1)}, u32[]{:S(2)}, u32[]{:S(2)}) %collective-permute-start.9) | collective-permute-done | bytes 360480 | tf_op jit(solution)/shard_map/ppermute | solution.py:57
  184.5 10.4 %collective-permute-start.12 = (bf16[3,16,704]{2,1,0:T(8,128)(2,1)S(1)}, bf16[3,16,704]{2,1,0:T(8,128)(2,1)S(1)}, u32[]{:S(2)}, u32[]{:S(2)}) collective-permute-start(bf16[3,16,704]{2,1,0:T(8,128)(2,1)S(1)} %fusion.93), channel_id=1, source_target_pairs={{8,0},{16,8},{24,16},{9,1},{17,9},{25,17},{10,2},{18,10},{26,18},{... | collective-permute-start | bytes 202760 | tf_op jit(solution)/shard_map/ppermute | solution.py:20
  194.9 1.9 collective-permute-start.11
  197.9 3.2 %collective-permute-done.11 = bf16[3,16,704]{2,1,0:T(8,128)(2,1)S(1)} collective-permute-done((bf16[3,16,704]{2,1,0:T(8,128)(2,1)S(1)}, bf16[3,16,704]{2,1,0:T(8,128)(2,1)S(1)}, u32[]{:S(2)}, u32[]{:S(2)}) %collective-permute-start.11) | collective-permute-done | bytes 67616 | tf_op jit(solution)/shard_map/ppermute | solution.py:17
  201.4 1.9 collective-permute-start.13
  203.3 2.4 %collective-permute-start.14 = (bf16[30,3,704]{2,1,0:T(4,128)(2,1)S(1)}, bf16[30,3,704]{2,1,0:T(4,128)(2,1)S(1)}, u32[]{:S(2)}, u32[]{:S(2)}) collective-permute-start(bf16[30,3,704]{2,1,0:T(4,128)(2,1)S(1)} %get-tuple-element.84), channel_id=1, source_target_pairs={{0,2},{2,4},{4,6},{1,3},{3,5},{5,7},{8,10},{10,12},{12,14},{9,11},... | collective-permute-start | bytes 380168 | tf_op jit(solution)/shard_map/ppermute | solution.py:17
  206.4 7.1 %collective-permute-done.14 = bf16[30,3,704]{2,1,0:T(4,128)(2,1)S(1)} collective-permute-done((bf16[30,3,704]{2,1,0:T(4,128)(2,1)S(1)}, bf16[30,3,704]{2,1,0:T(4,128)(2,1)S(1)}, u32[]{:S(2)}, u32[]{:S(2)}) %collective-permute-start.14) | collective-permute-done | bytes 126752 | tf_op jit(solution)/shard_map/ppermute | solution.py:17
  213.5 14.9 %add_convert_fusion.1 = bf16[24,16,704]{2,1,0:T(8,128)(2,1)} fusion(bf16[24,16,704]{2,1,0:T(8,128)(2,1)S(1)} %copy-done.1, bf16[30,16,704]{2,1,0:T(8,128)(2,1)S(1)} %constant_dynamic-update-slice_fusion.3, bf16[30,3,704]{2,1,0:T(4,128)(2,1)S(1)} %collective-permute-done.14, bf16[30,3,704]{2,1,0:T(4,128)(2,1)S(1)} %collective-permute-done.13, ...), kind=kLoop, calls=%fused_computation.130 | loop fusion | flops 77316096 | bytes 5933312 | tf_op jit(solution)/shard_map/convert_element_type | solution.py:196
  (99 shorter events, 26.8 us)
Async XLA Ops:
  7.2 24.6 %copy-start.1 = (bf16[24,16,704]{2,1,0:T(8,128)(2,1)S(1)}, bf16[24,16,704]{2,1,0:T(8,128)(2,1)}, u32[]{:S(2)}) copy-start(bf16[24,16,704]{2,1,0:T(8,128)(2,1)} %param.25) | copy-start | bytes 1622020
  7.2 74.8 %all-gather.2.cloned.1.call-start = ((), (), s32[]{:S(2)}) async-start(), calls=%async_computation | async-start | bytes 8425472 | tf_op jit(solution)/shard_map/all_gather | solution.py:99
  7.9 23.9 %copy-start.2 = (f32[7,7,704]{2,1,0:T(8,128)S(1)}, f32[7,7,704]{2,1,0:T(8,128)}, u32[]{:S(2)}) copy-start(f32[7,7,704]{2,1,0:T(8,128)} %param.14) | copy-start | bytes 413956
  8.9 23.2 %copy-start = (bf16[24,16,704]{2,1,0:T(8,128)(2,1)S(1)}, bf16[24,16,704]{2,1,0:T(8,128)(2,1)}, u32[]{:S(2)}) copy-start(bf16[24,16,704]{2,1,0:T(8,128)(2,1)} %param.13) | copy-start | bytes 1622020
  8.9 23.2 %collective-permute-start = (bf16[3,16,704]{2,1,0:T(8,128)(2,1)S(1)}, bf16[3,16,704]{2,1,0:T(8,128)(2,1)S(1)}, u32[]{:S(2)}, u32[]{:S(2)}) collective-permute-start(bf16[3,16,704]{2,1,0:T(8,128)(2,1)S(1)} %get-tuple-element.90), channel_id=1, source_target_pairs={{0,8},{8,16},{16,24},{1,9},{9,17},{17,25},{2,10},{10,18},{18,26},{... | collective-permute-start | bytes 202760 | tf_op jit(solution)/shard_map/ppermute | solution.py:17
  12.5 19.7 %collective-permute-start.1 = (bf16[3,16,704]{2,1,0:T(8,128)(2,1)S(1)}, bf16[3,16,704]{2,1,0:T(8,128)(2,1)S(1)}, u32[]{:S(2)}, u32[]{:S(2)}) collective-permute-start(bf16[3,16,704]{2,1,0:T(8,128)(2,1)S(1)} %get-tuple-element.89), channel_id=1, source_target_pairs={{8,0},{16,8},{24,16},{9,1},{17,9},{25,17},{10,2},{18,10},{26,18},{... | collective-permute-start | bytes 202760 | tf_op jit(solution)/shard_map/ppermute | solution.py:20
  32.4 6.9 %collective-permute-start.2 = (bf16[30,3,704]{2,1,0:T(4,128)(2,1)S(1)}, bf16[30,3,704]{2,1,0:T(4,128)(2,1)S(1)}, u32[]{:S(2)}, u32[]{:S(2)}) collective-permute-start(bf16[30,3,704]{2,1,0:T(4,128)(2,1)S(1)} %get-tuple-element.85), channel_id=1, source_target_pairs={{0,2},{2,4},{4,6},{1,3},{3,5},{5,7},{8,10},{10,12},{12,14},{9,11},... | collective-permute-start | bytes 380168 | tf_op jit(solution)/shard_map/ppermute | solution.py:17
  34.3 6.7 %collective-permute-start.3 = (bf16[30,3,704]{2,1,0:T(4,128)(2,1)S(1)}, bf16[30,3,704]{2,1,0:T(4,128)(2,1)S(1)}, u32[]{:S(2)}, u32[]{:S(2)}) collective-permute-start(bf16[30,3,704]{2,1,0:T(4,128)(2,1)S(1)} %get-tuple-element.86), channel_id=1, source_target_pairs={{2,0},{4,2},{6,4},{3,1},{5,3},{7,5},{10,8},{12,10},{14,12},{11,9},... | collective-permute-start | bytes 380168 | tf_op jit(solution)/shard_map/ppermute | solution.py:20
  48.8 13.4 %copy-start.6 = (f32[2816]{0:T(1024)S(1)}, f32[2816]{0:T(1024)}, u32[]{:S(2)}) copy-start(f32[2816]{0:T(1024)} %param.19) | copy-start | bytes 33796
  48.8 13.4 %copy-start.8 = (f32[1408]{0:T(1024)S(1)}, f32[1408]{0:T(1024)}, u32[]{:S(2)}) copy-start(f32[1408]{0:T(1024)} %param.17) | copy-start | bytes 16900
  48.8 12.1 %collective-permute-start.4 = (bf16[256,704]{1,0:T(8,128)(2,1)S(1)}, bf16[256,704]{1,0:T(8,128)(2,1)S(1)}, u32[]{:S(2)}, u32[]{:S(2)}) collective-permute-start(bf16[256,704]{1,0:T(8,128)(2,1)S(1)} %bitcast.67), channel_id=1, source_target_pairs={{0,1},{1,0},{2,3},{3,2},{4,5},{5,4},{6,7},{7,6},{8,9},{9,8},{10,11... | collective-permute-start | bytes 1081352 | tf_op jit(solution)/shard_map/ppermute | solution.py:57
  50.5 19.3 %collective-permute-start.7 = (bf16[256,704]{1,0:T(8,128)(2,1)S(1)}, bf16[256,704]{1,0:T(8,128)(2,1)S(1)}, u32[]{:S(2)}, u32[]{:S(2)}) collective-permute-start(bf16[256,704]{1,0:T(8,128)(2,1)S(1)} %fusion.29), channel_id=1, source_target_pairs={{0,1},{1,0},{2,3},{3,2},{4,5},{5,4},{6,7},{7,6},{8,9},{9,8},{10,11... | collective-permute-start | bytes 1081352 | tf_op jit(solution)/shard_map/ppermute | solution.py:57
  69.9 68.5 %copy-start.3 = (f32[2816]{0:T(1024)S(1)}, f32[2816]{0:T(1024)}, u32[]{:S(2)}) copy-start(f32[2816]{0:T(1024)} %param.20) | copy-start | bytes 33796
  69.9 89.9 %copy-start.7 = (f32[2816]{0:T(1024)S(1)}, f32[2816]{0:T(1024)}, u32[]{:S(2)}) copy-start(f32[2816]{0:T(1024)} %param.21) | copy-start | bytes 33796
  139.7 15.2 %collective-permute-start.5 = (f32[8,128]{1,0:T(8,128)S(1)}, f32[8,128]{1,0:T(8,128)S(1)}, u32[]{:S(2)}, u32[]{:S(2)}) collective-permute-start(f32[8,128]{1,0:T(8,128)S(1)} %broadcast_in_dim.16), channel_id=1, source_target_pairs={{0,1},{1,0},{2,3},{3,2},{4,5},{5,4},{6,7},{7,6},{8,9},{9,8},{10,11... | collective-permute-start | bytes 12296 | tf_op jit(solution)/shard_map/ppermute | solution.py:57
  154.2 3.7 %collective-permute-start.8 = (f32[8,128]{1,0:T(8,128)S(1)}, f32[8,128]{1,0:T(8,128)S(1)}, u32[]{:S(2)}, u32[]{:S(2)}) collective-permute-start(f32[8,128]{1,0:T(8,128)S(1)} %broadcast_in_dim.17), channel_id=1, source_target_pairs={{0,1},{1,0},{2,3},{3,2},{4,5},{5,4},{6,7},{7,6},{8,9},{9,8},{10,11... | collective-permute-start | bytes 12296 | tf_op jit(solution)/shard_map/ppermute | solution.py:57
  166.2 11.4 %collective-permute-start.6 = (bf16[256,704]{1,0:T(8,128)(2,1)S(1)}, bf16[256,704]{1,0:T(8,128)(2,1)S(1)}, u32[]{:S(2)}, u32[]{:S(2)}) collective-permute-start(bf16[256,704]{1,0:T(8,128)(2,1)S(1)} %dynamic-slice_convert_fusion.1), channel_id=1, source_target_pairs={{0,1},{1,0},{2,3},{3,2},{4,5},{5,4},{6,7},{7,6},{8,9},{9,8},{10,11... | collective-permute-start | bytes 1081352 | tf_op jit(solution)/shard_map/ppermute | solution.py:57
  167.0 16.4 %copy-start.5 = (f32[704]{0:T(1024)S(1)}, f32[704]{0:T(1024)}, u32[]{:S(2)}) copy-start(f32[704]{0:T(1024)} %param.23) | copy-start | bytes 8452
  173.9 3.7 %collective-permute-start.10 = (f32[2,256]{1,0:T(2,128)S(1)}, f32[2,256]{1,0:T(2,128)S(1)}, u32[]{:S(2)}, u32[]{:S(2)}) collective-permute-start(f32[2,256]{1,0:T(2,128)S(1)} %pad_maximum_fusion.8), channel_id=1, source_target_pairs={{0,1},{1,0},{2,3},{3,2},{4,5},{5,4},{6,7},{7,6},{8,9},{9,8},{10,11... | collective-permute-start | bytes 6152 | tf_op jit(solution)/shard_map/ppermute | solution.py:57
  175.5 7.8 %collective-permute-start.9 = (bf16[256,704]{1,0:T(8,128)(2,1)S(1)}, bf16[256,704]{1,0:T(8,128)(2,1)S(1)}, u32[]{:S(2)}, u32[]{:S(2)}) collective-permute-start(bf16[256,704]{1,0:T(8,128)(2,1)S(1)} %dynamic-slice_convert_fusion), channel_id=1, source_target_pairs={{0,1},{1,0},{2,3},{3,2},{4,5},{5,4},{6,7},{7,6},{8,9},{9,8},{10,11... | collective-permute-start | bytes 1081352 | tf_op jit(solution)/shard_map/ppermute | solution.py:57
  184.5 16.8 %collective-permute-start.12 = (bf16[3,16,704]{2,1,0:T(8,128)(2,1)S(1)}, bf16[3,16,704]{2,1,0:T(8,128)(2,1)S(1)}, u32[]{:S(2)}, u32[]{:S(2)}) collective-permute-start(bf16[3,16,704]{2,1,0:T(8,128)(2,1)S(1)} %fusion.93), channel_id=1, source_target_pairs={{8,0},{16,8},{24,16},{9,1},{17,9},{25,17},{10,2},{18,10},{26,18},{... | collective-permute-start | bytes 202760 | tf_op jit(solution)/shard_map/ppermute | solution.py:20
  194.9 6.2 %collective-permute-start.11 = (bf16[3,16,704]{2,1,0:T(8,128)(2,1)S(1)}, bf16[3,16,704]{2,1,0:T(8,128)(2,1)S(1)}, u32[]{:S(2)}, u32[]{:S(2)}) collective-permute-start(bf16[3,16,704]{2,1,0:T(8,128)(2,1)S(1)} %fusion.94), channel_id=1, source_target_pairs={{0,8},{8,16},{16,24},{1,9},{9,17},{17,25},{2,10},{10,18},{18,26},{... | collective-permute-start | bytes 202760 | tf_op jit(solution)/shard_map/ppermute | solution.py:17
  201.4 5.0 %collective-permute-start.13 = (bf16[30,3,704]{2,1,0:T(4,128)(2,1)S(1)}, bf16[30,3,704]{2,1,0:T(4,128)(2,1)S(1)}, u32[]{:S(2)}, u32[]{:S(2)}) collective-permute-start(bf16[30,3,704]{2,1,0:T(4,128)(2,1)S(1)} %get-tuple-element.83), channel_id=1, source_target_pairs={{2,0},{4,2},{6,4},{3,1},{5,3},{7,5},{10,8},{12,10},{14,12},{11,9},... | collective-permute-start | bytes 380168 | tf_op jit(solution)/shard_map/ppermute | solution.py:20
  203.3 10.2 %collective-permute-start.14 = (bf16[30,3,704]{2,1,0:T(4,128)(2,1)S(1)}, bf16[30,3,704]{2,1,0:T(4,128)(2,1)S(1)}, u32[]{:S(2)}, u32[]{:S(2)}) collective-permute-start(bf16[30,3,704]{2,1,0:T(4,128)(2,1)S(1)} %get-tuple-element.84), channel_id=1, source_target_pairs={{0,2},{2,4},{4,6},{1,3},{3,5},{5,7},{8,10},{10,12},{12,14},{9,11},... | collective-permute-start | bytes 380168 | tf_op jit(solution)/shard_map/ppermute | solution.py:17
  (5 other events, 35.7 us)
Sparse Core Ops, SparseCore 0:
  10.2 71.7 all-gather.1
where the time goes:
time: 236 us; the launch traced here: 235 us
  blocking collectives  48 us (20%)
  waiting for transfers between devices  43.9 us (19%)
  between operations  37.6 us (16%)
  starting transfers between devices  35.4 us (15%)
  other arithmetic  33.5 us (14%)
  matrix products  29.1 us (12%)
  local copies, waits for them, and re-layouts  7.66 us (3%)
    psum x1, blocking collectives, over_pixels(): return lax.psum(vector, ('sy', 'sx'))  48 us
    ppermute x4, starting transfers between devices, extended(): lax.ppermute(lax.slice_in_dim(block, 0, width, axis=dim), axis, backward)  18.3 us
    ppermute x7, waiting for transfers between devices, swapped(): return lax.ppermute(array, 'tp', [(i, count - 1 - i) for i in range(count)])  17.4 us
    convert_element_type x1, other arithmetic, shards(): feature_grad = (cotangent.astype(jnp.float32) + depthwise(extend(grad_ima...  14.9 us
    all_gather x1, waiting for transfers between devices, shards(): down_t = lax.all_gather(down_weight.T, ('sy', 'sx'), axis=0, tiled=True)  12.2 us
    ppermute x4, waiting for transfers between devices, extended(): lax.ppermute(lax.slice_in_dim(block, block.shape[dim] - width, None, axis...  11.4 us
    ppermute x4, starting transfers between devices, extended(): lax.ppermute(lax.slice_in_dim(block, block.shape[dim] - width, None, axis...  9.87 us
    dot_general x1, matrix products, shards(): back_hidden = jnp.dot(cot_wide, down_t, preferred_element_type=jnp.float32)  8.27 us
  transfers between devices with their start and end apart: 16, of which 10 were waited for; matrix products, arithmetic and copies ran while one was open for 15% of the time, Pallas kernels for 0%

commit v1 on v0

--- a/solution.py
+++ b/solution.py
@@ -7,6 +7,11 @@
 TILE = 8
 root_half = 0.7071067811865476
 root_two_pi_inv = 0.3989422804014327
+
+
+def add_all(x, name):
+    shards = lax.all_gather(x, name)
+    return jnp.sum(shards, axis=0)
 
 
 def extended(block, sides, width):
@@ -58,7 +63,7 @@
 
 
 def over_pixels(vector):
-    return lax.psum(vector, ("sy", "sx"))
+    return add_all(vector, ("sy", "sx"))
 
 
 def conv_tiles(windows, kernel):

time: 236 us -> 218 us (0.924)
  blocking collectives: 48 us -> 36.2 us
  starting transfers between devices: 35.4 us -> 30.1 us
    psum x1 -> x0, blocking collectives: 48 us -> none  [over_pixels(): return lax.psum(vector, ('sy', 'sx'))]
    all_gather x0 -> x2, blocking collectives: none -> 36.2 us  [add_all(): shards = lax.all_gather(x, name)]
    ppermute x4, starting transfers between devices: 18.3 us -> 13.1 us  [extended(): lax.ppermute(lax.slice_in_dim(block, 0, width, axis=dim), axis, backward)]
    ppermute x4, waiting for transfers between devices: 11.4 us -> 8.13 us  [extended(): lax.ppermute(lax.slice_in_dim(block, block.shape[dim] - width, None, axis...]
  transfers between devices with their start and end apart: 16 -> 16, of which waited for: 10 -> 10; matrix products, arithmetic and copies ran while one was open for 15% -> 17% of each run, Pallas kernels for 0% -> 0%
where the time goes in v1:
time: 218 us; the launch traced here: 217 us
  waiting for transfers between devices  42.3 us (19%)
  between operations  37.7 us (17%)
  blocking collectives  36.2 us (17%)
  other arithmetic  33.7 us (15%)
  starting transfers between devices  30.1 us (14%)
  matrix products  29.1 us (13%)
  local copies, waits for them, and re-layouts  7.69 us (4%)
    all_gather x2, blocking collectives, add_all(): shards = lax.all_gather(x, name)  36.2 us
    ppermute x7, waiting for transfers between devices, swapped(): return lax.ppermute(array, 'tp', [(i, count - 1 - i) for i in range(count)])  19 us
    convert_element_type x1, other arithmetic, shards(): feature_grad = (cotangent.astype(jnp.float32) + depthwise(extend(grad_ima...  14.9 us
    ppermute x4, starting transfers between devices, extended(): lax.ppermute(lax.slice_in_dim(block, 0, width, axis=dim), axis, backward)  13.1 us
    all_gather x1, waiting for transfers between devices, shards(): down_t = lax.all_gather(down_weight.T, ('sy', 'sx'), axis=0, tiled=True)  12.1 us
    ppermute x4, starting transfers between devices, extended(): lax.ppermute(lax.slice_in_dim(block, block.shape[dim] - width, None, axis...  9.87 us
    dot_general x1, matrix products, shards(): back_hidden = jnp.dot(cot_wide, down_t, preferred_element_type=jnp.float32)  8.26 us
    ppermute x4, waiting for transfers between devices, extended(): lax.ppermute(lax.slice_in_dim(block, block.shape[dim] - width, None, axis...  8.13 us
  transfers between devices with their start and end apart: 16, of which 10 were waited for; matrix products, arithmetic and copies ran while one was open for 17% of the time, Pallas kernels for 0%

profile of v1, /device:TPU:12, one launch (start us, length us, event | category | flops | bytes accessed | tf_op | source)
XLA Modules:
  0.0 216.7 jit_solution(18354878049924046646)
XLA Ops:
  8.9 3.6 %collective-permute-start = (bf16[3,16,704]{2,1,0:T(8,128)(2,1)S(1)}, bf16[3,16,704]{2,1,0:T(8,128)(2,1)S(1)}, u32[]{:S(2)}, u32[]{:S(2)}) collective-permute-start(bf16[3,16,704]{2,1,0:T(8,128)(2,1)S(1)} %get-tuple-element.88), channel_id=1, source_target_pairs={{0,8},{8,16},{16,24},{1,9},{9,17},{17,25},{2,10},{10,18},{18,26},{... | collective-permute-start | bytes 202760 | tf_op jit(solution)/shard_map/ppermute | solution.py:22
  12.5 2.4 %collective-permute-start.1 = (bf16[3,16,704]{2,1,0:T(8,128)(2,1)S(1)}, bf16[3,16,704]{2,1,0:T(8,128)(2,1)S(1)}, u32[]{:S(2)}, u32[]{:S(2)}) collective-permute-start(bf16[3,16,704]{2,1,0:T(8,128)(2,1)S(1)} %get-tuple-element.87), channel_id=1, source_target_pairs={{8,0},{16,8},{24,16},{9,1},{17,9},{25,17},{10,2},{18,10},{26,18},{... | collective-permute-start | bytes 202760 | tf_op jit(solution)/shard_map/ppermute | solution.py:25
  28.8 2.7 %add_convert_fusion.4 = f32[4]{0:T(128)S(1)} fusion(s32[1]{0:T(128)} %bitcast.3, s32[1]{0:T(128)} %bitcast.2, s32[1]{0:T(128)} %bitcast.1, s32[1]{0:T(128)} %bitcast), kind=kLoop, calls=%fused_computation.313 | loop fusion | flops 16 | bytes 32 | tf_op jit(solution)/shard_map/convert_element_type | solution.py:112
  32.4 1.9 collective-permute-start.2
  34.3 3.6 %collective-permute-start.3 = (bf16[30,3,704]{2,1,0:T(4,128)(2,1)S(1)}, bf16[30,3,704]{2,1,0:T(4,128)(2,1)S(1)}, u32[]{:S(2)}, u32[]{:S(2)}) collective-permute-start(bf16[30,3,704]{2,1,0:T(4,128)(2,1)S(1)} %get-tuple-element.84), channel_id=1, source_target_pairs={{2,0},{4,2},{6,4},{3,1},{5,3},{7,5},{10,8},{12,10},{14,12},{11,9},... | collective-permute-start | bytes 380168 | tf_op jit(solution)/shard_map/ppermute | solution.py:25
  39.2 1.8 collective-permute-done.3
  43.0 5.8 %add_convert_fusion.2 = bf16[4,8,8,704]{3,2,1,0:T(8,128)(2,1)S(1)} fusion(bf16[4,14,14,704]{3,2,1,0:T(8,128)(2,1)S(1)} %pad_maximum_fusion, f32[704]{0:T(1024)S(1)} %copy-done.4, f32[704]{0:T(1024)S(1)} %get-tuple-element.53, f32[704]{0:T(1024)S(1)} %get-tuple-element.54, f32[704]{0:T(1024)S(1)} %get-tuple-element.7, f32[704]{0:T(1024)S(1)} %get-tuple-element.8, ...), kind=kLoop, calls=%fused_computation.138 | loop fusion | flops 26673152 | bytes 18163200 | tf_op jit(solution)/shard_map/convert_element_type | solution.py:149
  48.8 1.6 collective-permute-start.4
  51.8 9.1 %collective-permute-done.4 = bf16[256,704]{1,0:T(8,128)(2,1)S(1)} collective-permute-done((bf16[256,704]{1,0:T(8,128)(2,1)S(1)}, bf16[256,704]{1,0:T(8,128)(2,1)S(1)}, u32[]{:S(2)}, u32[]{:S(2)}) %collective-permute-start.4) | collective-permute-done | bytes 360480 | tf_op jit(solution)/shard_map/ppermute | solution.py:62
  62.2 7.7 %convolution_add_fusion = f32[256,2816]{1,0:T(8,128)} fusion(bf16[1408,2816]{1,0:T(8,128)(2,1)} %param.18, f32[2816]{0:T(1024)S(1)} %copy-done.6, f32[1408]{0:T(1024)S(1)} %copy-done.8, f32[1408]{0:T(1024)S(1)} %copy-done.9, f32[256]{0:T(256)S(1)} %add_rsqrt_fusion, f32[256]{0:T(256)S(1)} %broadcast_multiply_fusion, bf16[256,704]{1,0:T(8,128)(2,1)S(1)} %bitcast.70, ...), kind=kOutput, calls=%fused_computation.47 | convolution fusion | flops 2036170752 | bytes 11558913 | tf_op jit(solution)/shard_map/dot_general | solution.py:156
  69.9 12.1 %all-gather.6.cloned.1.call-done = bf16[1408,2816]{1,0:T(8,128)(2,1)} async-done(((bf16[88,2816]{1,0:T(8,128)(2,1)}), bf16[1408,2816]{1,0:T(8,128)(2,1)}) %all-gather.6.cloned.1.call-update) | async-done | bytes 7929872 | tf_op jit(solution)/shard_map/all_gather | solution.py:104
  82.0 8.3 %fusion.10 = (f32[2816]{0:T(1024)S(1)}, f32[2816]{0:T(1024)S(1)}, bf16[256,2816]{1,0:T(8,128)(2,1)}, f32[256,2816]{1,0:T(8,128)}) fusion(f32[256]{0:T(256)S(1)} %convert_element_type.365, f32[256,2816]{1,0:T(8,128)} %convolution_add_fusion, bf16[1408,2816]{1,0:T(8,128)(2,1)} %all-gather.6.cloned.1.call-done, ...), kind=kOutput, calls=%fused_computation.58 | convolution fusion | flops 2041211392 | bytes 15883265 | tf_op jit(solution)/shard_map/dot_general | solution.py:164
  90.3 16.8 %all-gather.2 = f32[16,1,2816]{2,1,0:T(1,128)S(1)} all-gather(f32[1,1,2816]{2,1,0:T(1,128)S(1)} %reshape.145), channel_id=2, replica_groups=mesh['sy'=4,'sx'=4,'tp'=2] {'sy','sx'}, dimensions={0}, use_global_device_ids=true | all-gather | bytes 191488 | tf_op jit(solution)/shard_map/all_gather | solution.py:13
  107.0 19.5 %all-gather.3 = f32[16,1,2816]{2,1,0:T(1,128)S(1)} all-gather(f32[1,1,2816]{2,1,0:T(1,128)S(1)} %reshape.147), channel_id=3, replica_groups=mesh['sy'=4,'sx'=4,'tp'=2] {'sy','sx'}, dimensions={0}, use_global_device_ids=true | all-gather | bytes 191488 | tf_op jit(solution)/shard_map/all_gather | solution.py:13
  148.3 6.3 %fusion.16 = f32[256,1408]{1,0:T(8,128)S(1)} fusion(bf16[1408,2816]{1,0:T(8,128)(2,1)} %all-gather.6.cloned.1.call-done, bf16[256,2816]{1,0:T(8,128)(2,1)} %get-tuple-element.67, f32[2816]{0:T(1024)S(1)} %copy-done.7, f32[2816]{0:T(1024)S(1)} %get-tuple-element.66, f32[2816]{0:T(1024)S(1)} %copy-done.3), kind=kOutput, calls=%fused_computation.109 | convolution fusion | flops 2034368512 | bytes 10847232 | tf_op jit(solution)/shard_map/dot_general | solution.py:169
  155.4 6.9 %fusion.102 = (f32[256]{0:T(256)S(1)}, f32[256]{0:T(256)S(1)}, f32[256,1408]{1,0:T(8,128)S(1)}, f32[256,1408]{1,0:T(8,128)S(1)}) fusion(f32[256]{0:T(256)S(1)} %add_rsqrt_fusion, f32[256]{0:T(256)S(1)} %broadcast_multiply_fusion, bf16[256,704]{1,0:T(8,128)(2,1)S(1)} %bitcast.71, bf16[256,704]{1,0:T(8,128)(2,1)S(1)} %collective-permute-done.4, ...), kind=kOutput, calls=%fused_computation.322 | convolution fusion | flops 2047344128 | bytes 18787840 | tf_op jit(solution)/shard_map/dot_general | solution.py:184
  166.0 7.4 %collective-permute-done.9 = bf16[256,704]{1,0:T(8,128)(2,1)S(1)} collective-permute-done((bf16[256,704]{1,0:T(8,128)(2,1)S(1)}, bf16[256,704]{1,0:T(8,128)(2,1)S(1)}, u32[]{:S(2)}, u32[]{:S(2)}) %collective-permute-start.9) | collective-permute-done | bytes 360480 | tf_op jit(solution)/shard_map/ppermute | solution.py:62
  174.5 5.2 %collective-permute-start.12 = (bf16[3,16,704]{2,1,0:T(8,128)(2,1)S(1)}, bf16[3,16,704]{2,1,0:T(8,128)(2,1)S(1)}, u32[]{:S(2)}, u32[]{:S(2)}) collective-permute-start(bf16[3,16,704]{2,1,0:T(8,128)(2,1)S(1)} %fusion.93), channel_id=1, source_target_pairs={{8,0},{16,8},{24,16},{9,1},{17,9},{25,17},{10,2},{18,10},{26,18},{... | collective-permute-start | bytes 202760 | tf_op jit(solution)/shard_map/ppermute | solution.py:25
  179.7 1.9 collective-permute-start.11
  182.7 3.2 %collective-permute-done.11 = bf16[3,16,704]{2,1,0:T(8,128)(2,1)S(1)} collective-permute-done((bf16[3,16,704]{2,1,0:T(8,128)(2,1)S(1)}, bf16[3,16,704]{2,1,0:T(8,128)(2,1)S(1)}, u32[]{:S(2)}, u32[]{:S(2)}) %collective-permute-start.11) | collective-permute-done | bytes 67616 | tf_op jit(solution)/shard_map/ppermute | solution.py:22
  186.2 1.9 collective-permute-start.13
  188.1 2.4 %collective-permute-start.14 = (bf16[30,3,704]{2,1,0:T(4,128)(2,1)S(1)}, bf16[30,3,704]{2,1,0:T(4,128)(2,1)S(1)}, u32[]{:S(2)}, u32[]{:S(2)}) collective-permute-start(bf16[30,3,704]{2,1,0:T(4,128)(2,1)S(1)} %get-tuple-element.82), channel_id=1, source_target_pairs={{0,2},{2,4},{4,6},{1,3},{3,5},{5,7},{8,10},{10,12},{12,14},{9,11},... | collective-permute-start | bytes 380168 | tf_op jit(solution)/shard_map/ppermute | solution.py:22
  191.2 3.8 %collective-permute-done.14 = bf16[30,3,704]{2,1,0:T(4,128)(2,1)S(1)} collective-permute-done((bf16[30,3,704]{2,1,0:T(4,128)(2,1)S(1)}, bf16[30,3,704]{2,1,0:T(4,128)(2,1)S(1)}, u32[]{:S(2)}, u32[]{:S(2)}) %collective-permute-start.14) | collective-permute-done | bytes 126752 | tf_op jit(solution)/shard_map/ppermute | solution.py:22
  195.0 14.9 %add_convert_fusion.1 = bf16[24,16,704]{2,1,0:T(8,128)(2,1)} fusion(bf16[24,16,704]{2,1,0:T(8,128)(2,1)S(1)} %copy-done.1, bf16[30,16,704]{2,1,0:T(8,128)(2,1)S(1)} %constant_dynamic-update-slice_fusion.3, bf16[30,3,704]{2,1,0:T(4,128)(2,1)S(1)} %collective-permute-done.14, bf16[30,3,704]{2,1,0:T(4,128)(2,1)S(1)} %collective-permute-done.13, ...), kind=kLoop, calls=%fused_computation.130 | loop fusion | flops 77316096 | bytes 5933312 | tf_op jit(solution)/shard_map/convert_element_type | solution.py:201
  (104 shorter events, 28.4 us)
Async XLA Ops:
  7.2 24.6 %copy-start.1 = (bf16[24,16,704]{2,1,0:T(8,128)(2,1)S(1)}, bf16[24,16,704]{2,1,0:T(8,128)(2,1)}, u32[]{:S(2)}) copy-start(bf16[24,16,704]{2,1,0:T(8,128)(2,1)} %param.25) | copy-start | bytes 1622020
  7.2 74.8 %all-gather.6.cloned.1.call-start = ((), (), s32[]{:S(2)}) async-start(), calls=%async_computation | async-start | bytes 8425472 | tf_op jit(solution)/shard_map/all_gather | solution.py:104
  7.9 23.9 %copy-start.2 = (f32[7,7,704]{2,1,0:T(8,128)S(1)}, f32[7,7,704]{2,1,0:T(8,128)}, u32[]{:S(2)}) copy-start(f32[7,7,704]{2,1,0:T(8,128)} %param.14) | copy-start | bytes 413956
  8.9 23.2 %copy-start = (bf16[24,16,704]{2,1,0:T(8,128)(2,1)S(1)}, bf16[24,16,704]{2,1,0:T(8,128)(2,1)}, u32[]{:S(2)}) copy-start(bf16[24,16,704]{2,1,0:T(8,128)(2,1)} %param.13) | copy-start | bytes 1622020
  8.9 23.2 %collective-permute-start = (bf16[3,16,704]{2,1,0:T(8,128)(2,1)S(1)}, bf16[3,16,704]{2,1,0:T(8,128)(2,1)S(1)}, u32[]{:S(2)}, u32[]{:S(2)}) collective-permute-start(bf16[3,16,704]{2,1,0:T(8,128)(2,1)S(1)} %get-tuple-element.88), channel_id=1, source_target_pairs={{0,8},{8,16},{16,24},{1,9},{9,17},{17,25},{2,10},{10,18},{18,26},{... | collective-permute-start | bytes 202760 | tf_op jit(solution)/shard_map/ppermute | solution.py:22
  12.5 19.7 %collective-permute-start.1 = (bf16[3,16,704]{2,1,0:T(8,128)(2,1)S(1)}, bf16[3,16,704]{2,1,0:T(8,128)(2,1)S(1)}, u32[]{:S(2)}, u32[]{:S(2)}) collective-permute-start(bf16[3,16,704]{2,1,0:T(8,128)(2,1)S(1)} %get-tuple-element.87), channel_id=1, source_target_pairs={{8,0},{16,8},{24,16},{9,1},{17,9},{25,17},{10,2},{18,10},{26,18},{... | collective-permute-start | bytes 202760 | tf_op jit(solution)/shard_map/ppermute | solution.py:25
  32.4 6.9 %collective-permute-start.2 = (bf16[30,3,704]{2,1,0:T(4,128)(2,1)S(1)}, bf16[30,3,704]{2,1,0:T(4,128)(2,1)S(1)}, u32[]{:S(2)}, u32[]{:S(2)}) collective-permute-start(bf16[30,3,704]{2,1,0:T(4,128)(2,1)S(1)} %get-tuple-element.83), channel_id=1, source_target_pairs={{0,2},{2,4},{4,6},{1,3},{3,5},{5,7},{8,10},{10,12},{12,14},{9,11},... | collective-permute-start | bytes 380168 | tf_op jit(solution)/shard_map/ppermute | solution.py:22
  34.3 6.7 %collective-permute-start.3 = (bf16[30,3,704]{2,1,0:T(4,128)(2,1)S(1)}, bf16[30,3,704]{2,1,0:T(4,128)(2,1)S(1)}, u32[]{:S(2)}, u32[]{:S(2)}) collective-permute-start(bf16[30,3,704]{2,1,0:T(4,128)(2,1)S(1)} %get-tuple-element.84), channel_id=1, source_target_pairs={{2,0},{4,2},{6,4},{3,1},{5,3},{7,5},{10,8},{12,10},{14,12},{11,9},... | collective-permute-start | bytes 380168 | tf_op jit(solution)/shard_map/ppermute | solution.py:25
  48.8 13.4 %copy-start.6 = (f32[2816]{0:T(1024)S(1)}, f32[2816]{0:T(1024)}, u32[]{:S(2)}) copy-start(f32[2816]{0:T(1024)} %param.19) | copy-start | bytes 33796
  48.8 13.4 %copy-start.8 = (f32[1408]{0:T(1024)S(1)}, f32[1408]{0:T(1024)}, u32[]{:S(2)}) copy-start(f32[1408]{0:T(1024)} %param.17) | copy-start | bytes 16900
  48.8 12.1 %collective-permute-start.4 = (bf16[256,704]{1,0:T(8,128)(2,1)S(1)}, bf16[256,704]{1,0:T(8,128)(2,1)S(1)}, u32[]{:S(2)}, u32[]{:S(2)}) collective-permute-start(bf16[256,704]{1,0:T(8,128)(2,1)S(1)} %bitcast.67), channel_id=1, source_target_pairs={{0,1},{1,0},{2,3},{3,2},{4,5},{5,4},{6,7},{7,6},{8,9},{9,8},{10,11... | collective-permute-start | bytes 1081352 | tf_op jit(solution)/shard_map/ppermute | solution.py:62
  50.5 19.3 %collective-permute-start.7 = (bf16[256,704]{1,0:T(8,128)(2,1)S(1)}, bf16[256,704]{1,0:T(8,128)(2,1)S(1)}, u32[]{:S(2)}, u32[]{:S(2)}) collective-permute-start(bf16[256,704]{1,0:T(8,128)(2,1)S(1)} %fusion.29), channel_id=1, source_target_pairs={{0,1},{1,0},{2,3},{3,2},{4,5},{5,4},{6,7},{7,6},{8,9},{9,8},{10,11... | collective-permute-start | bytes 1081352 | tf_op jit(solution)/shard_map/ppermute | solution.py:62
  69.9 56.9 %copy-start.3 = (f32[2816]{0:T(1024)S(1)}, f32[2816]{0:T(1024)}, u32[]{:S(2)}) copy-start(f32[2816]{0:T(1024)} %param.20) | copy-start | bytes 33796
  69.9 78.4 %copy-start.7 = (f32[2816]{0:T(1024)S(1)}, f32[2816]{0:T(1024)}, u32[]{:S(2)}) copy-start(f32[2816]{0:T(1024)} %param.21) | copy-start | bytes 33796
  128.1 15.2 %collective-permute-start.5 = (f32[8,128]{1,0:T(8,128)S(1)}, f32[8,128]{1,0:T(8,128)S(1)}, u32[]{:S(2)}, u32[]{:S(2)}) collective-permute-start(f32[8,128]{1,0:T(8,128)S(1)} %broadcast_in_dim.16), channel_id=1, source_target_pairs={{0,1},{1,0},{2,3},{3,2},{4,5},{5,4},{6,7},{7,6},{8,9},{9,8},{10,11... | collective-permute-start | bytes 12296 | tf_op jit(solution)/shard_map/ppermute | solution.py:62
  142.7 3.7 %collective-permute-start.8 = (f32[8,128]{1,0:T(8,128)S(1)}, f32[8,128]{1,0:T(8,128)S(1)}, u32[]{:S(2)}, u32[]{:S(2)}) collective-permute-start(f32[8,128]{1,0:T(8,128)S(1)} %broadcast_in_dim.17), channel_id=1, source_target_pairs={{0,1},{1,0},{2,3},{3,2},{4,5},{5,4},{6,7},{7,6},{8,9},{9,8},{10,11... | collective-permute-start | bytes 12296 | tf_op jit(solution)/shard_map/ppermute | solution.py:62
  154.7 11.3 %collective-permute-start.6 = (bf16[256,704]{1,0:T(8,128)(2,1)S(1)}, bf16[256,704]{1,0:T(8,128)(2,1)S(1)}, u32[]{:S(2)}, u32[]{:S(2)}) collective-permute-start(bf16[256,704]{1,0:T(8,128)(2,1)S(1)} %dynamic-slice_convert_fusion.1), channel_id=1, source_target_pairs={{0,1},{1,0},{2,3},{3,2},{4,5},{5,4},{6,7},{7,6},{8,9},{9,8},{10,11... | collective-permute-start | bytes 1081352 | tf_op jit(solution)/shard_map/ppermute | solution.py:62
  155.4 18.0 %copy-start.5 = (f32[704]{0:T(1024)S(1)}, f32[704]{0:T(1024)}, u32[]{:S(2)}) copy-start(f32[704]{0:T(1024)} %param.23) | copy-start | bytes 8452
  162.3 3.7 %collective-permute-start.10 = (f32[2,256]{1,0:T(2,128)S(1)}, f32[2,256]{1,0:T(2,128)S(1)}, u32[]{:S(2)}, u32[]{:S(2)}) collective-permute-start(f32[2,256]{1,0:T(2,128)S(1)} %pad_maximum_fusion.8), channel_id=1, source_target_pairs={{0,1},{1,0},{2,3},{3,2},{4,5},{5,4},{6,7},{7,6},{8,9},{9,8},{10,11... | collective-permute-start | bytes 6152 | tf_op jit(solution)/shard_map/ppermute | solution.py:62
  164.0 9.5 %collective-permute-start.9 = (bf16[256,704]{1,0:T(8,128)(2,1)S(1)}, bf16[256,704]{1,0:T(8,128)(2,1)S(1)}, u32[]{:S(2)}, u32[]{:S(2)}) collective-permute-start(bf16[256,704]{1,0:T(8,128)(2,1)S(1)} %dynamic-slice_convert_fusion), channel_id=1, source_target_pairs={{0,1},{1,0},{2,3},{3,2},{4,5},{5,4},{6,7},{7,6},{8,9},{9,8},{10,11... | collective-permute-start | bytes 1081352 | tf_op jit(solution)/shard_map/ppermute | solution.py:62
  174.5 11.5 %collective-permute-start.12 = (bf16[3,16,704]{2,1,0:T(8,128)(2,1)S(1)}, bf16[3,16,704]{2,1,0:T(8,128)(2,1)S(1)}, u32[]{:S(2)}, u32[]{:S(2)}) collective-permute-start(bf16[3,16,704]{2,1,0:T(8,128)(2,1)S(1)} %fusion.93), channel_id=1, source_target_pairs={{8,0},{16,8},{24,16},{9,1},{17,9},{25,17},{10,2},{18,10},{26,18},{... | collective-permute-start | bytes 202760 | tf_op jit(solution)/shard_map/ppermute | solution.py:25
  179.7 6.2 %collective-permute-start.11 = (bf16[3,16,704]{2,1,0:T(8,128)(2,1)S(1)}, bf16[3,16,704]{2,1,0:T(8,128)(2,1)S(1)}, u32[]{:S(2)}, u32[]{:S(2)}) collective-permute-start(bf16[3,16,704]{2,1,0:T(8,128)(2,1)S(1)} %fusion.94), channel_id=1, source_target_pairs={{0,8},{8,16},{16,24},{1,9},{9,17},{17,25},{2,10},{10,18},{18,26},{... | collective-permute-start | bytes 202760 | tf_op jit(solution)/shard_map/ppermute | solution.py:22
  186.2 5.0 %collective-permute-start.13 = (bf16[30,3,704]{2,1,0:T(4,128)(2,1)S(1)}, bf16[30,3,704]{2,1,0:T(4,128)(2,1)S(1)}, u32[]{:S(2)}, u32[]{:S(2)}) collective-permute-start(bf16[30,3,704]{2,1,0:T(4,128)(2,1)S(1)} %get-tuple-element.81), channel_id=1, source_target_pairs={{2,0},{4,2},{6,4},{3,1},{5,3},{7,5},{10,8},{12,10},{14,12},{11,9},... | collective-permute-start | bytes 380168 | tf_op jit(solution)/shard_map/ppermute | solution.py:25
  188.1 6.9 %collective-permute-start.14 = (bf16[30,3,704]{2,1,0:T(4,128)(2,1)S(1)}, bf16[30,3,704]{2,1,0:T(4,128)(2,1)S(1)}, u32[]{:S(2)}, u32[]{:S(2)}) collective-permute-start(bf16[30,3,704]{2,1,0:T(4,128)(2,1)S(1)} %get-tuple-element.82), channel_id=1, source_target_pairs={{0,2},{2,4},{4,6},{1,3},{3,5},{5,7},{8,10},{10,12},{12,14},{9,11},... | collective-permute-start | bytes 380168 | tf_op jit(solution)/shard_map/ppermute | solution.py:22
  (5 other events, 35.6 us)
Sparse Core Ops, SparseCore 0:
  10.2 71.7 all-gather.5
